TPU v7x, 32 devices: a whole 2x2x4 slice. The times are simulated.
32 devices in a mesh: phase: 2 (over x), ctx: 16 (over z, y, core).
Axes of the slice: x: 2, y: 2, z: 4, core: 2. Of those that a mesh axis runs over, the one named last changes fastest.
Arguments:
- embed: bfloat16 [2048, 4096], P('ctx'), may hold values from -6 to 6
- gains: float32 [2, 4096], P('phase'), may hold values from 0.1 to 1.9
- keys: bfloat16 [2, 2048, 1024], P('phase', 'ctx'), may hold values from -512 to 512
- values: bfloat16 [2, 2048, 1024], P('phase', 'ctx'), may hold values from -6 to 6
- block_order: int32 [16], replicated, may hold values from 0 to 15, each once
- block_doc: int32 [16], replicated, may hold values from 0 to 3, never falling along the last dimension, each value on 1 to 8 neighbouring positions
Outputs:
- phase_output: bfloat16 [2, 2048, 4096], P('phase', 'ctx')
Inputs may be any that keep to these rules, and one draw needn't show every extreme that they name: Storage block b of every token-indexed array holds the sequence's block block_order[b]. `block_doc`: documents are numbered in sequence order and never fall; each covers 1 to 8 whole blocks, one exactly 8.
All inputs are finite; a program needn't handle non-finite values.
Results may differ from a plain program's by a relative error of at most 0.0063.
Values may be sent and summed in bfloat16 or wider, within the bound.
A program may use at most 128 MiB of HBM per device.

v0:
```python
import functools
import math

import jax
import jax.numpy as jnp
from jax import lax
from jax.experimental import pallas as pl
from jax.experimental.pallas import tpu as pltpu
from jax.sharding import PartitionSpec as P

HEADS = 32
KVH = 8
HDIM = 128
REP = HEADS // KVH
QW = REP * HDIM
NEG = -1e30
MESH = pl.DeviceIdType.MESH


def kernel(
    layers, ctx, block,
    order_ref, doc_ref, embed_ref, gains_ref, keys_ref, values_ref,
    out_ref,
    kv, hbuf, gbuf, obuf, qbuf, mbuf, lbuf, acc, ss_send, ss_recv,
    loc_sem, kv_send, kv_recv, e_send, e_recv, g_send, g_recv,
    s_send, s_recv, z_send, z_recv, o_send, o_recv,
):
    split = KVH // layers
    groups = ctx // split
    p = lax.axis_index("phase")
    c = lax.axis_index("ctx")
    g = lax.rem(c, split)
    z = lax.div(c, split)
    k = p * split + g
    width = embed_ref.shape[1]

    def device_of(head, group):
        return (lax.div(head, split), group * split + lax.rem(head, split))

    def peer(i):
        return lax.rem(k + i, KVH)

    barrier = pltpu.get_barrier_semaphore()
    for i in range(1, KVH):
        pl.semaphore_signal(barrier, inc=1, device_id=device_of(peer(i), z), device_id_type=MESH)

    @pl.when(z > 0)
    def _():
        pl.semaphore_signal(barrier, inc=1, device_id=(p, c - split), device_id_type=MESH)

    @pl.when(z < groups - 1)
    def _():
        pl.semaphore_signal(barrier, inc=1, device_id=(p, c + split), device_id_type=MESH)

    count = KVH - 1 + (z > 0).astype(jnp.int32) + (z < groups - 1).astype(jnp.int32)
    pl.semaphore_wait(barrier, count)

    def cols(head, size):
        return pl.ds(pl.multiple_of(head * size, size), size)

    def remote(src, dst, send, recv, device):
        return pltpu.make_async_remote_copy(
            src_ref=src, dst_ref=dst, send_sem=send, recv_sem=recv,
            device_id=device, device_id_type=MESH,
        )

    def kv_copy(i, which):
        source = (keys_ref, values_ref)[which]
        return remote(
            source.at[0, :, cols(peer(i), HDIM)], kv.at[p, z, g, which],
            kv_send.at[i, which], kv_recv.at[p, g, which], device_of(peer(i), z),
        )

    def kv_arrive(layer, b, which):
        spot = kv.at[layer, z, b, which]
        return remote(spot, spot, kv_send.at[0, which], kv_recv.at[layer, b, which], (p, c))

    def e_copy(i):
        other = lax.rem(g + i, split)
        return remote(
            embed_ref.at[:, cols(p * split + other, QW)], hbuf.at[g],
            e_send.at[i], e_recv.at[g], (p, z * split + other),
        )

    def g_copy(i):
        other = lax.rem(p + i, layers)
        return remote(
            gains_ref.at[:, cols(other * split + g, QW)], gbuf.at[p],
            g_send.at[i], g_recv.at[p], (other, c),
        )

    locals_ = [
        pltpu.make_async_copy(keys_ref.at[0, :, cols(k, HDIM)], kv.at[p, z, g, 0], loc_sem.at[0]),
        pltpu.make_async_copy(values_ref.at[0, :, cols(k, HDIM)], kv.at[p, z, g, 1], loc_sem.at[1]),
        pltpu.make_async_copy(embed_ref.at[:, cols(k, QW)], hbuf.at[g], loc_sem.at[2]),
        pltpu.make_async_copy(gains_ref.at[:, cols(k, QW)], gbuf.at[p], loc_sem.at[3]),
    ]
    for copy in locals_:
        copy.start()
    for i in range(1, KVH):
        kv_copy(i, 0).start()
        kv_copy(i, 1).start()
    for i in range(1, split):
        e_copy(i).start()
    for i in range(1, layers):
        g_copy(i).start()
    for copy in locals_:
        copy.wait()

    def z_copy(layer, src, b, up):
        spot = kv.at[layer, src, b]
        step = split if up else -split
        return remote(
            spot, spot, z_send.at[layer, src, int(up), b], z_recv.at[layer, src, b], (p, c + step)
        )

    def wait_chunk(layer, b):
        @pl.when(jnp.logical_not((p == layer) & (g == b)))
        def _():
            kv_arrive(layer, b, 0).wait_recv()
            kv_arrive(layer, b, 1).wait_recv()

    def send_chunk(layer, src, b, up):
        @pl.when(z < groups - 1 if up else z > 0)
        def _():
            z_copy(layer, src, b, up).start()

    for i in range(split):
        b = lax.rem(g + i, split)
        wait_chunk(0, b)
        send_chunk(0, z, b, True)
        send_chunk(0, z, b, False)

    for i in range(1, split):
        b = lax.rem(g + i, split)
        remote(hbuf.at[b], hbuf.at[b], e_send.at[0], e_recv.at[b], (p, c)).wait_recv()
    for i in range(1, layers):
        other = lax.rem(p + i, layers)
        remote(gbuf.at[other], gbuf.at[other], g_send.at[0], g_recv.at[other], (p, c)).wait_recv()

    lane = lax.broadcasted_iota(jnp.int32, (block, 128), 1)
    diff = lane - lax.broadcasted_iota(jnp.int32, (block, 128), 0)
    factor = math.log2(math.e) / math.sqrt(HDIM)

    def s_copy(layer, i):
        return remote(
            ss_send.at[layer], ss_recv.at[layer, k],
            s_send.at[layer, i], s_recv.at[layer, k], device_of(peer(i), z),
        )

    def make_queries(layer):
        def hidden(j):
            return (hbuf[j] if layer == 0 else obuf[layer - 1, j]).astype(jnp.float32)

        partial = jnp.zeros((block, 128), jnp.float32)
        for j in range(split):
            wide = hidden(j)
            partial = jnp.where(lane == j, jnp.sum(wide * wide, axis=1, keepdims=True), partial)
        turned = partial.T[:8]
        ss_send[layer] = turned
        ss_recv[layer, k] = turned
        for i in range(1, KVH):
            s_copy(layer, i).start()
        for i in range(1, KVH):
            other = peer(i)
            spot = ss_recv.at[layer, other]
            remote(spot, spot, s_send.at[layer, 0], s_recv.at[layer, other], (p, c)).wait_recv()
        total = jnp.sum(ss_recv[layer], axis=0)
        scale = lax.rsqrt(total * (1.0 / width) + 1e-05)
        scale = jnp.concatenate([scale] * (block // 8), axis=0).T
        for j in range(split):
            queries = (hidden(j) * scale[:, j:j + 1] * gbuf[layer]).astype(jnp.bfloat16)
            for i in range(REP):
                qbuf[j, i * block:(i + 1) * block, :] = queries[:, i * HDIM:(i + 1) * HDIM]

    def attend(layer, src, first):
        key_tile = kv[layer, src, :, 0].reshape(split * block, HDIM)
        value_tile = kv[layer, src, :, 1].reshape(split * block, HDIM)

        def rows(j, carry):
            scores = lax.dot_general(
                qbuf[j], key_tile, (((1,), (1,)), ((), ())), preferred_element_type=jnp.float32
            )
            own = order_ref[z * split + j]
            own_doc = doc_ref[own]
            parts = []
            for b in range(split):
                other = order_ref[src * split + b]
                limit = jnp.where(doc_ref[other] == own_doc, (own - other) * block, -(1 << 24))
                bias = jnp.where(diff <= limit, 0.0, NEG)
                part = scores[:, b * block:(b + 1) * block].reshape(REP, block, block)
                parts.append((part * factor + bias[None]).reshape(REP * block, block))
            top = functools.reduce(jnp.maximum, parts)
            top = jnp.max(top, axis=1, keepdims=True)
            if not first:
                old = mbuf[j]
                top = jnp.maximum(old, top)
            else:
                top = jnp.broadcast_to(top, (REP * block, 128))
            expo = [jnp.exp2(part - top) for part in parts]
            added = functools.reduce(jnp.add, expo)
            weights = jnp.concatenate([e.astype(jnp.bfloat16) for e in expo], axis=1)
            product = jnp.dot(weights, value_tile, preferred_element_type=jnp.float32)
            mbuf[j] = top
            if first:
                lbuf[j] = added
                acc[j] = product
            else:
                shrink = jnp.exp2(old - top)
                lbuf[j] = lbuf[j] * shrink + added
                acc[j] = acc[j] * shrink + product
            return carry

        lax.fori_loop(0, split, rows, 0)

    def o_copy(layer, j):
        return remote(
            obuf.at[layer, j], out_ref.at[0, :, cols(k, QW)],
            o_send.at[layer, j], o_recv.at[k], (layer, z * split + j),
        )

    def o_local(layer, j):
        return pltpu.make_async_copy(
            obuf.at[layer, j], out_ref.at[0, :, cols(k, QW)], o_send.at[layer, j]
        )

    def finish(layer):
        for j in range(split):
            wide = (hbuf[j] if layer == 0 else obuf[layer - 1, j]).astype(jnp.float32)
            total = jnp.sum(lbuf[j], axis=1, keepdims=True)
            attended = (acc[j] / total).astype(jnp.bfloat16).astype(jnp.float32)
            for i in range(REP):
                span = slice(i * HDIM, (i + 1) * HDIM)
                obuf[layer, j, :, span] = (
                    wide[:, span] + attended[i * block:(i + 1) * block]
                ).astype(jnp.bfloat16)
            mine = (p == layer) & (g == j)

            @pl.when(mine)
            def _():
                o_local(layer, j).start()

            @pl.when(jnp.logical_not(mine))
            def _():
                o_copy(layer, j).start()

    def send_next(layer, t):
        if layer + 1 == layers:
            return

        @pl.when(z == t)
        def _():
            for b in range(split):
                send_chunk(layer + 1, z, b, True)

        @pl.when(groups - 1 - z == t)
        def _():
            for b in range(split):
                send_chunk(layer + 1, z, b, False)

    for layer in range(layers):
        make_queries(layer)
        attend(layer, z, True)
        if layer == 0:
            for later in range(1, layers):
                for b in range(split):
                    wait_chunk(later, b)
        send_next(layer, 0)

        def step(t, carry):
            below, above = z - t, z + t

            @pl.when(below >= 0)
            def _():
                for b in range(split):
                    z_copy(layer, below, b, True).wait_recv()
                    send_chunk(layer, below, b, True)

            @pl.when(above < groups)
            def _():
                for b in range(split):
                    z_copy(layer, above, b, False).wait_recv()
                    send_chunk(layer, above, b, False)

            send_next(layer, t)

            @pl.when(below >= 0)
            def _():
                attend(layer, below, False)

            @pl.when(above < groups)
            def _():
                attend(layer, above, False)

            return carry

        lax.fori_loop(1, groups, step, 0)
        finish(layer)

    for i in range(1, KVH):
        kv_copy(i, 0).wait_send()
        kv_copy(i, 1).wait_send()
    for i in range(1, split):
        e_copy(i).wait_send()
    for i in range(1, layers):
        g_copy(i).wait_send()
    for layer in range(layers):
        for i in range(1, KVH):
            s_copy(layer, i).wait_send()

        def drain(src, carry):
            @pl.when((src <= z) & (z < groups - 1))
            def _():
                for b in range(split):
                    z_copy(layer, src, b, True).wait_send()

            @pl.when((src >= z) & (z > 0))
            def _():
                for b in range(split):
                    z_copy(layer, src, b, False).wait_send()

            return carry

        lax.fori_loop(0, groups, drain, 0)
        for j in range(split):
            mine = (p == layer) & (g == j)

            @pl.when(mine)
            def _():
                o_local(layer, j).wait()

            @pl.when(jnp.logical_not(mine))
            def _():
                o_copy(layer, j).wait_send()

    for i in range(1, KVH):
        other = peer(i)
        spot = out_ref.at[0, :, cols(other, QW)]
        remote(spot, spot, o_send.at[0, 0], o_recv.at[other], (p, c)).wait_recv()


def body(layers, ctx, embed, gains, keys, values, block_order, block_doc):
    block, width = embed.shape
    split = KVH // layers
    groups = ctx // split
    dma = pltpu.SemaphoreType.DMA
    smem = pl.BlockSpec(memory_space=pltpu.SMEM)
    anywhere = pl.BlockSpec(memory_space=pl.ANY)
    rows = REP * block
    return pl.pallas_call(
        functools.partial(kernel, layers, ctx, block),
        out_shape=jax.ShapeDtypeStruct((1, block, width), jnp.bfloat16),
        in_specs=[smem, smem] + [anywhere] * 4,
        out_specs=anywhere,
        scratch_shapes=[
            pltpu.VMEM((layers, groups, split, 2, block, HDIM), jnp.bfloat16),
            pltpu.VMEM((split, block, QW), jnp.bfloat16),
            pltpu.VMEM((layers, 1, QW), jnp.float32),
            pltpu.VMEM((layers, split, block, QW), jnp.bfloat16),
            pltpu.VMEM((split, rows, HDIM), jnp.bfloat16),
            pltpu.VMEM((split, rows, 128), jnp.float32),
            pltpu.VMEM((split, rows, 128), jnp.float32),
            pltpu.VMEM((split, rows, HDIM), jnp.float32),
            pltpu.VMEM((layers, 8, 128), jnp.float32),
            pltpu.VMEM((layers, KVH, 8, 128), jnp.float32),
            dma((4,)),
            dma((KVH, 2)),
            dma((layers, split, 2)),
            dma((split,)),
            dma((split,)),
            dma((layers,)),
            dma((layers,)),
            dma((layers, KVH)),
            dma((layers, KVH)),
            dma((layers, groups, 2, split)),
            dma((layers, groups, split)),
            dma((layers, split)),
            dma((KVH,)),
        ],
        compiler_params=pltpu.CompilerParams(
            collective_id=0, has_side_effects=True, vmem_limit_bytes=48 * 1024 * 1024
        ),
    )(block_order, block_doc, embed, gains, keys, values)


def solution(mesh):
    placed = (
        P("ctx", None),
        P("phase", None),
        P("phase", "ctx", None),
        P("phase", "ctx", None),
        P(),
        P(),
    )
    run = functools.partial(body, mesh.shape["phase"], mesh.shape["ctx"])
    return jax.shard_map(
        run, mesh=mesh, in_specs=placed, out_specs=P("phase", "ctx", None), check_vma=False
    )
```

profile of v0, /device:TPU:0, one launch (start us, length us, event | category | flops | bytes accessed | tf_op | source)
XLA Modules:
  0.0 86.6 jit_solution(4438007904686717966)
XLA Ops:
  0.0 0.0 copy-start
  0.0 1.2 %copy-done = bf16[128,4096]{1,0:T(8,128)(2,1)S(1)} copy-done((bf16[128,4096]{1,0:T(8,128)(2,1)S(1)}, bf16[128,4096]{1,0:T(8,128)(2,1)}, u32[]{:S(2)}) %copy-start) | copy-done | bytes 1048600
  1.2 0.0 copy-start.1
  1.2 0.9 %copy-done.1 = bf16[1,128,1024]{2,1,0:T(8,128)(2,1)S(1)} copy-done((bf16[1,128,1024]{2,1,0:T(8,128)(2,1)S(1)}, bf16[1,128,1024]{2,1,0:T(8,128)(2,1)}, u32[]{:S(2)}) %copy-start.1) | copy-done | bytes 262168
  2.2 0.0 copy-start.2
  2.2 0.9 %copy-done.2 = bf16[1,128,1024]{2,1,0:T(8,128)(2,1)S(1)} copy-done((bf16[1,128,1024]{2,1,0:T(8,128)(2,1)S(1)}, bf16[1,128,1024]{2,1,0:T(8,128)(2,1)}, u32[]{:S(2)}) %copy-start.2) | copy-done | bytes 262168
  3.1 0.0 copy-start.3
  3.1 0.7 copy-done.3
  3.8 0.0 copy-start.4
  3.8 0.7 copy-done.4
  4.5 0.0 copy-start.5
  4.5 0.7 copy-done.5
  5.2 80.5 %shard_map.64 = bf16[1,128,4096]{2,1,0:T(8,128)(2,1)S(1)} custom-call(s32[16]{0:T(128)S(1)} %copy-done.4, s32[16]{0:T(128)S(1)} %copy-done.5, bf16[128,4096]{1,0:T(8,128)(2,1)S(1)} %copy-done, f32[1,4096]{1,0:T(1,128)S(1)} %copy-done.3, bf16[1,128,1024]{2,1,0:T(8,128)(2,1)S(1)} %copy-done.1, bf16[1,128,1024]{2,1,0:T(8,128)(2,1)S(1)} %copy-done.2), custom_call_target="tpu_custom_call" | custom-call | tf_op jit(solution)/shard_map/pallas_call | solution.py:350
  85.7 1.0 %copy.8 = bf16[1,128,4096]{2,1,0:T(8,128)(2,1)} copy(bf16[1,128,4096]{2,1,0:T(8,128)(2,1)S(1)} %shard_map.64) | data formatting | bytes 2097152
Async XLA Ops:
  0.0 1.2 %copy-start = (bf16[128,4096]{1,0:T(8,128)(2,1)S(1)}, bf16[128,4096]{1,0:T(8,128)(2,1)}, u32[]{:S(2)}) copy-start(bf16[128,4096]{1,0:T(8,128)(2,1)} %embed_ref.1) | copy-start | bytes 3145732
  1.2 0.9 %copy-start.1 = (bf16[1,128,1024]{2,1,0:T(8,128)(2,1)S(1)}, bf16[1,128,1024]{2,1,0:T(8,128)(2,1)}, u32[]{:S(2)}) copy-start(bf16[1,128,1024]{2,1,0:T(8,128)(2,1)} %keys_ref.1) | copy-start | bytes 786436
  2.2 0.9 %copy-start.2 = (bf16[1,128,1024]{2,1,0:T(8,128)(2,1)S(1)}, bf16[1,128,1024]{2,1,0:T(8,128)(2,1)}, u32[]{:S(2)}) copy-start(bf16[1,128,1024]{2,1,0:T(8,128)(2,1)} %values_ref.1) | copy-start | bytes 786436
  3.1 0.7 copy-start.3
  3.8 0.7 copy-start.4
  4.5 0.7 copy-start.5
where the time goes:
time: 86.9 us; the launch traced here: 86.6 us
  Pallas kernels  80.5 us (93%)
  local copies, waits for them, and re-layouts  6.12 us (7%)
    pallas_call x1, Pallas kernels, body(): pl.pallas_call(functools.partial(kernel, layers, ctx, block), out_shape=j...  80.5 us
    unnamed x13, local copies, waits for them, and re-layouts  6.12 us

commit v1 on v0

--- a/solution.py
+++ b/solution.py
@@ -21,9 +21,9 @@
     layers, ctx, block,
     order_ref, doc_ref, embed_ref, gains_ref, keys_ref, values_ref,
     out_ref,
-    kv, hbuf, gbuf, obuf, qbuf, mbuf, lbuf, acc, ss_send, ss_recv,
+    kv, hbuf, gbuf, obuf, qbuf, mbuf, lbuf, acc, ss_send, ss_recv, kst, est, rbuf,
     loc_sem, kv_send, kv_recv, e_send, e_recv, g_send, g_recv,
-    s_send, s_recv, z_send, z_recv, o_send, o_recv,
+    s_send, s_recv, z_send, z_recv, o_send, o_recv, st_sem, e_st_sem, r_sem,
 ):
     split = KVH // layers
     groups = ctx // split
@@ -64,23 +64,30 @@
             device_id=device, device_id_type=MESH,
         )
 
-    def kv_copy(i, which):
+    def kv_stage(i, which):
         source = (keys_ref, values_ref)[which]
+        return pltpu.make_async_copy(
+            source.at[0, :, cols(peer(i), HDIM)], kst.at[i, which], st_sem.at[i, which]
+        )
+
+    def kv_copy(i):
         return remote(
-            source.at[0, :, cols(peer(i), HDIM)], kv.at[p, z, g, which],
-            kv_send.at[i, which], kv_recv.at[p, g, which], device_of(peer(i), z),
-        )
-
-    def kv_arrive(layer, b, which):
-        spot = kv.at[layer, z, b, which]
-        return remote(spot, spot, kv_send.at[0, which], kv_recv.at[layer, b, which], (p, c))
+            kst.at[i], kv.at[p, z, g], kv_send.at[i], kv_recv.at[p, g], device_of(peer(i), z)
+        )
+
+    def kv_arrive(layer, b):
+        spot = kv.at[layer, z, b]
+        return remote(spot, spot, kv_send.at[0], kv_recv.at[layer, b], (p, c))
+
+    def e_stage(i):
+        other = lax.rem(g + i, split)
+        return pltpu.make_async_copy(
+            embed_ref.at[:, cols(p * split + other, QW)], est.at[i], e_st_sem.at[i]
+        )
 
     def e_copy(i):
         other = lax.rem(g + i, split)
-        return remote(
-            embed_ref.at[:, cols(p * split + other, QW)], hbuf.at[g],
-            e_send.at[i], e_recv.at[g], (p, z * split + other),
-        )
+        return remote(est.at[i], hbuf.at[g], e_send.at[i], e_recv.at[g], (p, z * split + other))
 
     def g_copy(i):
         other = lax.rem(p + i, layers)
@@ -98,9 +105,16 @@
     for copy in locals_:
         copy.start()
     for i in range(1, KVH):
-        kv_copy(i, 0).start()
-        kv_copy(i, 1).start()
+        kv_stage(i, 0).start()
+        kv_stage(i, 1).start()
     for i in range(1, split):
+        e_stage(i).start()
+    for i in range(1, KVH):
+        kv_stage(i, 0).wait()
+        kv_stage(i, 1).wait()
+        kv_copy(i).start()
+    for i in range(1, split):
+        e_stage(i).wait()
         e_copy(i).start()
     for i in range(1, layers):
         g_copy(i).start()
@@ -117,8 +131,7 @@
     def wait_chunk(layer, b):
         @pl.when(jnp.logical_not((p == layer) & (g == b)))
         def _():
-            kv_arrive(layer, b, 0).wait_recv()
-            kv_arrive(layer, b, 1).wait_recv()
+            kv_arrive(layer, b).wait_recv()
 
     def send_chunk(layer, src, b, up):
         @pl.when(z < groups - 1 if up else z > 0)
@@ -211,11 +224,11 @@
                 acc[j] = acc[j] * shrink + product
             return carry
 
-        lax.fori_loop(0, split, rows, 0)
+        lax.fori_loop(0, split, rows, 0, unroll=True)
 
     def o_copy(layer, j):
         return remote(
-            obuf.at[layer, j], out_ref.at[0, :, cols(k, QW)],
+            obuf.at[layer, j], rbuf.at[k],
             o_send.at[layer, j], o_recv.at[k], (layer, z * split + j),
         )
 
@@ -298,8 +311,7 @@
         finish(layer)
 
     for i in range(1, KVH):
-        kv_copy(i, 0).wait_send()
-        kv_copy(i, 1).wait_send()
+        kv_copy(i).wait_send()
     for i in range(1, split):
         e_copy(i).wait_send()
     for i in range(1, layers):
@@ -333,10 +345,17 @@
             def _():
                 o_copy(layer, j).wait_send()
 
-    for i in range(1, KVH):
-        other = peer(i)
-        spot = out_ref.at[0, :, cols(other, QW)]
-        remote(spot, spot, o_send.at[0, 0], o_recv.at[other], (p, c)).wait_recv()
+    def place(i):
+        return pltpu.make_async_copy(
+            rbuf.at[peer(i)], out_ref.at[0, :, cols(peer(i), QW)], r_sem.at[i]
+        )
+
+    for i in range(1, KVH):
+        spot = rbuf.at[peer(i)]
+        remote(spot, spot, o_send.at[0, 0], o_recv.at[peer(i)], (p, c)).wait_recv()
+        place(i).start()
+    for i in range(1, KVH):
+        place(i).wait()
 
 
 def body(layers, ctx, embed, gains, keys, values, block_order, block_doc):
@@ -363,9 +382,12 @@
             pltpu.VMEM((split, rows, HDIM), jnp.float32),
             pltpu.VMEM((layers, 8, 128), jnp.float32),
             pltpu.VMEM((layers, KVH, 8, 128), jnp.float32),
+            pltpu.VMEM((KVH, 2, block, HDIM), jnp.bfloat16),
+            pltpu.VMEM((split, block, QW), jnp.bfloat16),
+            pltpu.VMEM((KVH, block, QW), jnp.bfloat16),
             dma((4,)),
-            dma((KVH, 2)),
-            dma((layers, split, 2)),
+            dma((KVH,)),
+            dma((layers, split)),
             dma((split,)),
             dma((split,)),
             dma((layers,)),
@@ -375,6 +397,9 @@
             dma((layers, groups, 2, split)),
             dma((layers, groups, split)),
             dma((layers, split)),
+            dma((KVH,)),
+            dma((KVH, 2)),
+            dma((split,)),
             dma((KVH,)),
         ],
         compiler_params=pltpu.CompilerParams(

time: 86.9 us -> 83.4 us (0.960)
  Pallas kernels: 80.5 us -> 76.9 us
    pallas_call x1, Pallas kernels: 80.5 us -> 76.9 us  [body(): pl.pallas_call(functools.partial(kernel, layers, ctx, block), out_shape=j...]
where the time goes in v1:
time: 83.4 us; the launch traced here: 83.1 us
  Pallas kernels  76.9 us (92%)
  local copies, waits for them, and re-layouts  6.12 us (7%)
    pallas_call x1, Pallas kernels, body(): pl.pallas_call(functools.partial(kernel, layers, ctx, block), out_shape=j...  76.9 us
    unnamed x13, local copies, waits for them, and re-layouts  6.12 us

profile of v1, /device:TPU:0, one launch (start us, length us, event | category | flops | bytes accessed | tf_op | source)
XLA Modules:
  0.0 83.1 jit_solution(7689276911246619765)
XLA Ops:
  0.0 0.0 copy-start
  0.0 1.2 %copy-done = bf16[128,4096]{1,0:T(8,128)(2,1)S(1)} copy-done((bf16[128,4096]{1,0:T(8,128)(2,1)S(1)}, bf16[128,4096]{1,0:T(8,128)(2,1)}, u32[]{:S(2)}) %copy-start) | copy-done | bytes 1048600
  1.2 0.0 copy-start.1
  1.2 0.9 %copy-done.1 = bf16[1,128,1024]{2,1,0:T(8,128)(2,1)S(1)} copy-done((bf16[1,128,1024]{2,1,0:T(8,128)(2,1)S(1)}, bf16[1,128,1024]{2,1,0:T(8,128)(2,1)}, u32[]{:S(2)}) %copy-start.1) | copy-done | bytes 262168
  2.2 0.0 copy-start.2
  2.2 0.9 %copy-done.2 = bf16[1,128,1024]{2,1,0:T(8,128)(2,1)S(1)} copy-done((bf16[1,128,1024]{2,1,0:T(8,128)(2,1)S(1)}, bf16[1,128,1024]{2,1,0:T(8,128)(2,1)}, u32[]{:S(2)}) %copy-start.2) | copy-done | bytes 262168
  3.1 0.0 copy-start.3
  3.1 0.7 copy-done.3
  3.8 0.0 copy-start.4
  3.8 0.7 copy-done.4
  4.5 0.0 copy-start.5
  4.5 0.7 copy-done.5
  5.2 76.9 %shard_map.64 = bf16[1,128,4096]{2,1,0:T(8,128)(2,1)S(1)} custom-call(s32[16]{0:T(128)S(1)} %copy-done.4, s32[16]{0:T(128)S(1)} %copy-done.5, bf16[128,4096]{1,0:T(8,128)(2,1)S(1)} %copy-done, f32[1,4096]{1,0:T(1,128)S(1)} %copy-done.3, bf16[1,128,1024]{2,1,0:T(8,128)(2,1)S(1)} %copy-done.1, bf16[1,128,1024]{2,1,0:T(8,128)(2,1)S(1)} %copy-done.2), custom_call_target="tpu_custom_call" | custom-call | tf_op jit(solution)/shard_map/pallas_call | solution.py:369
  82.1 1.0 %copy.8 = bf16[1,128,4096]{2,1,0:T(8,128)(2,1)} copy(bf16[1,128,4096]{2,1,0:T(8,128)(2,1)S(1)} %shard_map.64) | data formatting | bytes 2097152
Async XLA Ops:
  0.0 1.2 %copy-start = (bf16[128,4096]{1,0:T(8,128)(2,1)S(1)}, bf16[128,4096]{1,0:T(8,128)(2,1)}, u32[]{:S(2)}) copy-start(bf16[128,4096]{1,0:T(8,128)(2,1)} %embed_ref.1) | copy-start | bytes 3145732
  1.2 0.9 %copy-start.1 = (bf16[1,128,1024]{2,1,0:T(8,128)(2,1)S(1)}, bf16[1,128,1024]{2,1,0:T(8,128)(2,1)}, u32[]{:S(2)}) copy-start(bf16[1,128,1024]{2,1,0:T(8,128)(2,1)} %keys_ref.1) | copy-start | bytes 786436
  2.2 0.9 %copy-start.2 = (bf16[1,128,1024]{2,1,0:T(8,128)(2,1)S(1)}, bf16[1,128,1024]{2,1,0:T(8,128)(2,1)}, u32[]{:S(2)}) copy-start(bf16[1,128,1024]{2,1,0:T(8,128)(2,1)} %values_ref.1) | copy-start | bytes 786436
  3.1 0.7 copy-start.3
  3.8 0.7 copy-start.4
  4.5 0.7 copy-start.5

commit v2 on v1

--- a/solution.py
+++ b/solution.py
@@ -186,11 +186,11 @@
             for i in range(REP):
                 qbuf[j, i * block:(i + 1) * block, :] = queries[:, i * HDIM:(i + 1) * HDIM]
 
-    def attend(layer, src, first):
+    def attend(layer, src, first, last=False):
         key_tile = kv[layer, src, :, 0].reshape(split * block, HDIM)
         value_tile = kv[layer, src, :, 1].reshape(split * block, HDIM)
 
-        def rows(j, carry):
+        def rows(j):
             scores = lax.dot_general(
                 qbuf[j], key_tile, (((1,), (1,)), ((), ())), preferred_element_type=jnp.float32
             )
@@ -222,9 +222,12 @@
                 shrink = jnp.exp2(old - top)
                 lbuf[j] = lbuf[j] * shrink + added
                 acc[j] = acc[j] * shrink + product
-            return carry
-
-        lax.fori_loop(0, split, rows, 0, unroll=True)
+
+        for i in range(split):
+            j = lax.rem(g + 1 + i, split)
+            rows(j)
+            if last:
+                finish(layer, j, i == split - 1)
 
     def o_copy(layer, j):
         return remote(
@@ -237,25 +240,25 @@
             obuf.at[layer, j], out_ref.at[0, :, cols(k, QW)], o_send.at[layer, j]
         )
 
-    def finish(layer):
-        for j in range(split):
-            wide = (hbuf[j] if layer == 0 else obuf[layer - 1, j]).astype(jnp.float32)
-            total = jnp.sum(lbuf[j], axis=1, keepdims=True)
-            attended = (acc[j] / total).astype(jnp.bfloat16).astype(jnp.float32)
-            for i in range(REP):
-                span = slice(i * HDIM, (i + 1) * HDIM)
-                obuf[layer, j, :, span] = (
-                    wide[:, span] + attended[i * block:(i + 1) * block]
-                ).astype(jnp.bfloat16)
-            mine = (p == layer) & (g == j)
-
-            @pl.when(mine)
+    def finish(layer, j, at_home):
+        wide = (hbuf[j] if layer == 0 else obuf[layer - 1, j]).astype(jnp.float32)
+        total = jnp.sum(lbuf[j], axis=1, keepdims=True)
+        attended = (acc[j] / total).astype(jnp.bfloat16).astype(jnp.float32)
+        for i in range(REP):
+            span = slice(i * HDIM, (i + 1) * HDIM)
+            obuf[layer, j, :, span] = (
+                wide[:, span] + attended[i * block:(i + 1) * block]
+            ).astype(jnp.bfloat16)
+        if at_home:
+            @pl.when(p == layer)
             def _():
                 o_local(layer, j).start()
 
-            @pl.when(jnp.logical_not(mine))
+            @pl.when(p != layer)
             def _():
                 o_copy(layer, j).start()
+        else:
+            o_copy(layer, j).start()
 
     def send_next(layer, t):
         if layer + 1 == layers:
@@ -273,7 +276,7 @@
 
     for layer in range(layers):
         make_queries(layer)
-        attend(layer, z, True)
+        attend(layer, z, True, groups == 1)
         if layer == 0:
             for later in range(1, layers):
                 for b in range(split):
@@ -297,18 +300,24 @@
 
             send_next(layer, t)
 
-            @pl.when(below >= 0)
+            ends = t == jnp.maximum(z, groups - 1 - z)
+            ends_below = ends & (above >= groups)
+
+            @pl.when((below >= 0) & jnp.logical_not(ends_below))
             def _():
                 attend(layer, below, False)
 
-            @pl.when(above < groups)
+            @pl.when((above < groups) & jnp.logical_not(ends))
             def _():
                 attend(layer, above, False)
 
+            @pl.when(ends)
+            def _():
+                attend(layer, jnp.where(above < groups, above, below), False, True)
+
             return carry
 
         lax.fori_loop(1, groups, step, 0)
-        finish(layer)
 
     for i in range(1, KVH):
         kv_copy(i).wait_send()

time: 83.4 us -> 80.5 us (0.965)
  Pallas kernels: 76.9 us -> 74.1 us
    pallas_call x1, Pallas kernels: 76.9 us -> 74.1 us  [body(): pl.pallas_call(functools.partial(kernel, layers, ctx, block), out_shape=j...]
where the time goes in v2:
time: 80.5 us; the launch traced here: 80.3 us
  Pallas kernels  74.1 us (92%)
  local copies, waits for them, and re-layouts  6.12 us (8%)
    pallas_call x1, Pallas kernels, body(): pl.pallas_call(functools.partial(kernel, layers, ctx, block), out_shape=j...  74.1 us
    unnamed x13, local copies, waits for them, and re-layouts  6.12 us

profile of v2, /device:TPU:0, one launch (start us, length us, event | category | flops | bytes accessed | tf_op | source)
XLA Modules:
  0.0 80.3 jit_solution(12406438859054675919)
XLA Ops:
  0.0 0.0 copy-start
  0.0 1.2 %copy-done = bf16[128,4096]{1,0:T(8,128)(2,1)S(1)} copy-done((bf16[128,4096]{1,0:T(8,128)(2,1)S(1)}, bf16[128,4096]{1,0:T(8,128)(2,1)}, u32[]{:S(2)}) %copy-start) | copy-done | bytes 1048600
  1.2 0.0 copy-start.1
  1.2 0.9 %copy-done.1 = bf16[1,128,1024]{2,1,0:T(8,128)(2,1)S(1)} copy-done((bf16[1,128,1024]{2,1,0:T(8,128)(2,1)S(1)}, bf16[1,128,1024]{2,1,0:T(8,128)(2,1)}, u32[]{:S(2)}) %copy-start.1) | copy-done | bytes 262168
  2.2 0.0 copy-start.2
  2.2 0.9 %copy-done.2 = bf16[1,128,1024]{2,1,0:T(8,128)(2,1)S(1)} copy-done((bf16[1,128,1024]{2,1,0:T(8,128)(2,1)S(1)}, bf16[1,128,1024]{2,1,0:T(8,128)(2,1)}, u32[]{:S(2)}) %copy-start.2) | copy-done | bytes 262168
  3.1 0.0 copy-start.3
  3.1 0.7 copy-done.3
  3.8 0.0 copy-start.4
  3.8 0.7 copy-done.4
  4.5 0.0 copy-start.5
  4.5 0.7 copy-done.5
  5.2 74.1 %shard_map.64 = bf16[1,128,4096]{2,1,0:T(8,128)(2,1)S(1)} custom-call(s32[16]{0:T(128)S(1)} %copy-done.4, s32[16]{0:T(128)S(1)} %copy-done.5, bf16[128,4096]{1,0:T(8,128)(2,1)S(1)} %copy-done, f32[1,4096]{1,0:T(1,128)S(1)} %copy-done.3, bf16[1,128,1024]{2,1,0:T(8,128)(2,1)S(1)} %copy-done.1, bf16[1,128,1024]{2,1,0:T(8,128)(2,1)S(1)} %copy-done.2), custom_call_target="tpu_custom_call" | custom-call | tf_op jit(solution)/shard_map/pallas_call | solution.py:378
  79.3 1.0 %copy.8 = bf16[1,128,4096]{2,1,0:T(8,128)(2,1)} copy(bf16[1,128,4096]{2,1,0:T(8,128)(2,1)S(1)} %shard_map.64) | data formatting | bytes 2097152
Async XLA Ops:
  0.0 1.2 %copy-start = (bf16[128,4096]{1,0:T(8,128)(2,1)S(1)}, bf16[128,4096]{1,0:T(8,128)(2,1)}, u32[]{:S(2)}) copy-start(bf16[128,4096]{1,0:T(8,128)(2,1)} %embed_ref.1) | copy-start | bytes 3145732
  1.2 0.9 %copy-start.1 = (bf16[1,128,1024]{2,1,0:T(8,128)(2,1)S(1)}, bf16[1,128,1024]{2,1,0:T(8,128)(2,1)}, u32[]{:S(2)}) copy-start(bf16[1,128,1024]{2,1,0:T(8,128)(2,1)} %keys_ref.1) | copy-start | bytes 786436
  2.2 0.9 %copy-start.2 = (bf16[1,128,1024]{2,1,0:T(8,128)(2,1)S(1)}, bf16[1,128,1024]{2,1,0:T(8,128)(2,1)}, u32[]{:S(2)}) copy-start(bf16[1,128,1024]{2,1,0:T(8,128)(2,1)} %values_ref.1) | copy-start | bytes 786436
  3.1 0.7 copy-start.3
  3.8 0.7 copy-start.4
  4.5 0.7 copy-start.5

commit v3 on v2

--- a/solution.py
+++ b/solution.py
@@ -274,31 +274,41 @@
             for b in range(split):
                 send_chunk(layer + 1, z, b, False)
 
+    def forward(layer, t):
+        below, above = z - t, z + t
+
+        @pl.when(below >= 0)
+        def _():
+            for b in range(split):
+                z_copy(layer, below, b, True).wait_recv()
+                send_chunk(layer, below, b, True)
+
+        @pl.when(above < groups)
+        def _():
+            for b in range(split):
+                z_copy(layer, above, b, False).wait_recv()
+                send_chunk(layer, above, b, False)
+
+        send_next(layer, t)
+
     for layer in range(layers):
+        if layer > 0:
+            send_next(layer, 0)
+            forward(layer, 1)
         make_queries(layer)
         attend(layer, z, True, groups == 1)
         if layer == 0:
             for later in range(1, layers):
                 for b in range(split):
                     wait_chunk(later, b)
-        send_next(layer, 0)
+            send_next(layer, 0)
 
         def step(t, carry):
             below, above = z - t, z + t
 
-            @pl.when(below >= 0)
-            def _():
-                for b in range(split):
-                    z_copy(layer, below, b, True).wait_recv()
-                    send_chunk(layer, below, b, True)
-
-            @pl.when(above < groups)
-            def _():
-                for b in range(split):
-                    z_copy(layer, above, b, False).wait_recv()
-                    send_chunk(layer, above, b, False)
-
-            send_next(layer, t)
+            @pl.when(t > (0 if layer == 0 else 1))
+            def _():
+                forward(layer, t)
 
             ends = t == jnp.maximum(z, groups - 1 - z)
             ends_below = ends & (above >= groups)

time: 80.5 us -> 78.8 us (0.979)
  Pallas kernels: 74.1 us -> 72.4 us
    pallas_call x1, Pallas kernels: 74.1 us -> 72.4 us  [body(): pl.pallas_call(functools.partial(kernel, layers, ctx, block), out_shape=j...]
where the time goes in v3:
time: 78.8 us; the launch traced here: 78.5 us
  Pallas kernels  72.4 us (92%)
  local copies, waits for them, and re-layouts  6.12 us (8%)
    pallas_call x1, Pallas kernels, body(): pl.pallas_call(functools.partial(kernel, layers, ctx, block), out_shape=j...  72.4 us
    unnamed x13, local copies, waits for them, and re-layouts  6.12 us

profile of v3, /device:TPU:0, one launch (start us, length us, event | category | flops | bytes accessed | tf_op | source)
XLA Modules:
  0.0 78.5 jit_solution(4329856345255749760)
XLA Ops:
  0.0 0.0 copy-start
  0.0 1.2 %copy-done = bf16[128,4096]{1,0:T(8,128)(2,1)S(1)} copy-done((bf16[128,4096]{1,0:T(8,128)(2,1)S(1)}, bf16[128,4096]{1,0:T(8,128)(2,1)}, u32[]{:S(2)}) %copy-start) | copy-done | bytes 1048600
  1.2 0.0 copy-start.1
  1.2 0.9 %copy-done.1 = bf16[1,128,1024]{2,1,0:T(8,128)(2,1)S(1)} copy-done((bf16[1,128,1024]{2,1,0:T(8,128)(2,1)S(1)}, bf16[1,128,1024]{2,1,0:T(8,128)(2,1)}, u32[]{:S(2)}) %copy-start.1) | copy-done | bytes 262168
  2.2 0.0 copy-start.2
  2.2 0.9 %copy-done.2 = bf16[1,128,1024]{2,1,0:T(8,128)(2,1)S(1)} copy-done((bf16[1,128,1024]{2,1,0:T(8,128)(2,1)S(1)}, bf16[1,128,1024]{2,1,0:T(8,128)(2,1)}, u32[]{:S(2)}) %copy-start.2) | copy-done | bytes 262168
  3.1 0.0 copy-start.3
  3.1 0.7 copy-done.3
  3.8 0.0 copy-start.4
  3.8 0.7 copy-done.4
  4.5 0.0 copy-start.5
  4.5 0.7 copy-done.5
  5.2 72.4 %shard_map.64 = bf16[1,128,4096]{2,1,0:T(8,128)(2,1)S(1)} custom-call(s32[16]{0:T(128)S(1)} %copy-done.4, s32[16]{0:T(128)S(1)} %copy-done.5, bf16[128,4096]{1,0:T(8,128)(2,1)S(1)} %copy-done, f32[1,4096]{1,0:T(1,128)S(1)} %copy-done.3, bf16[1,128,1024]{2,1,0:T(8,128)(2,1)S(1)} %copy-done.1, bf16[1,128,1024]{2,1,0:T(8,128)(2,1)S(1)} %copy-done.2), custom_call_target="tpu_custom_call" | custom-call | tf_op jit(solution)/shard_map/pallas_call | solution.py:388
  77.6 1.0 %copy.8 = bf16[1,128,4096]{2,1,0:T(8,128)(2,1)} copy(bf16[1,128,4096]{2,1,0:T(8,128)(2,1)S(1)} %shard_map.64) | data formatting | bytes 2097152
Async XLA Ops:
  0.0 1.2 %copy-start = (bf16[128,4096]{1,0:T(8,128)(2,1)S(1)}, bf16[128,4096]{1,0:T(8,128)(2,1)}, u32[]{:S(2)}) copy-start(bf16[128,4096]{1,0:T(8,128)(2,1)} %embed_ref.1) | copy-start | bytes 3145732
  1.2 0.9 %copy-start.1 = (bf16[1,128,1024]{2,1,0:T(8,128)(2,1)S(1)}, bf16[1,128,1024]{2,1,0:T(8,128)(2,1)}, u32[]{:S(2)}) copy-start(bf16[1,128,1024]{2,1,0:T(8,128)(2,1)} %keys_ref.1) | copy-start | bytes 786436
  2.2 0.9 %copy-start.2 = (bf16[1,128,1024]{2,1,0:T(8,128)(2,1)S(1)}, bf16[1,128,1024]{2,1,0:T(8,128)(2,1)}, u32[]{:S(2)}) copy-start(bf16[1,128,1024]{2,1,0:T(8,128)(2,1)} %values_ref.1) | copy-start | bytes 786436
  3.1 0.7 copy-start.3
  3.8 0.7 copy-start.4
  4.5 0.7 copy-start.5
